TPU v7x, 32 devices: a whole 2x2x4 slice. The times are simulated.
32 devices in a mesh: grp: 2 (over y), row: 4 (over z), col: 2 (over x), sub: 2 (over core).
Axes of the slice: x: 2, y: 2, z: 4, core: 2. Of those that a mesh axis runs over, the one named last changes fastest.
Arguments:
- filament_slot: int32 [16384], P(('grp', 'row', 'col', 'sub')), parts along dimension 0, may hold values from 0 to 8191, each once
- wire_radius: float32 [16384], P(('grp', 'row', 'col', 'sub')), parts along dimension 0, may hold values from 0.02 to 0.05
- strand_radius: float32 [128], P('grp'), parts along dimension 0, may hold values from 0.2 to 1
- test_matrix: float32 [64, 16384], P(None, ('grp', 'row', 'col', 'sub')), parts along dimension 1, may hold values from -6 to 6
Outputs:
- ortho_basis: float32 [64, 16384], P(None, ('grp', 'row', 'col', 'sub')), parts along dimension 1
- sketch_factor: float32 [128, 64], P('grp'), parts along dimension 0
There are 2 independent parts, one for each index of `grp`. A program takes and returns all parts, laid end to end along the dimension named above; each array names one. Nothing has to cross between parts.
Inputs may be any that keep to these rules, and one draw needn't show every extreme that they name: `filament_slot`: every number from 0 to 8191 occurs exactly once.
All inputs are finite; a program needn't handle non-finite values.
Results may differ from a plain program's by a relative error of at most 0.0005.
Values sent between devices are 32-bit elements; how exact they have to be, the bound alone decides.
A program may use at most 64 MiB of HBM per device.

v0:
```python
import math

import jax
import jax.numpy as jnp
from jax import lax
from jax.sharding import PartitionSpec as P

SEGMENTS = 128


mu_scale = 1e-05
twist_rate = 4.0 * math.pi


def from_behind(shard, axis, by):
    count = lax.axis_size(axis)
    return lax.ppermute(shard, axis, [(i, (i + by) % count) for i in range(count)])


def filament_geometry(filament_slot, wire_radius, strand_radius):
    strand = filament_slot // SEGMENTS
    segment = filament_slot % SEGMENTS
    strand_count = strand_radius.shape[0]
    onehot = (strand[None, :] == jnp.arange(strand_count, dtype=jnp.int32)[:, None]).astype(
        jnp.float32
    )
    radius = jnp.sum(onehot * strand_radius[:, None], axis=0)
    phase = 2.0 * math.pi / strand_count * strand.astype(jnp.float32)
    height = (segment.astype(jnp.float32) + 0.5) / SEGMENTS
    twist_angle = phase + twist_rate * height
    cosine_part = jnp.cos(twist_angle)
    sine_part = jnp.sin(twist_angle)
    return jnp.stack(
        [
            radius * cosine_part,
            radius * sine_part,
            height,
            -twist_rate * radius * sine_part,
            twist_rate * radius * cosine_part,
            jnp.ones_like(height),
            wire_radius * wire_radius,
        ]
    )


def source_block(targets, sources, columns):
    delta_x = sources[0][:, None] - targets[0][None, :]
    delta_y = sources[1][:, None] - targets[1][None, :]
    delta_z = sources[2][:, None] - targets[2][None, :]
    distance = (
        delta_x * delta_x
        + delta_y * delta_y
        + delta_z * delta_z
        + sources[6][:, None]
        + targets[6][None, :]
    )
    alignment = (
        sources[3][:, None] * targets[3][None, :]
        + sources[4][:, None] * targets[4][None, :]
        + sources[5][:, None] * targets[5][None, :]
    )
    kernel = mu_scale * alignment * lax.rsqrt(distance)
    return jnp.dot(
        columns, kernel, precision=lax.Precision.HIGHEST, preferred_element_type=jnp.float32
    )


def sweep_sources(targets, sources, columns):
    source_count = sources.shape[1]
    block_len = math.gcd(source_count, 2048)
    block_count = source_count // block_len
    if block_count == 1:
        return source_block(targets, sources, columns)

    def add_block(block_index, running):
        offset = block_index * block_len
        geo_part = lax.dynamic_slice_in_dim(sources, offset, block_len, 1)
        col_part = lax.dynamic_slice_in_dim(columns, offset, block_len, 1)
        return running + source_block(targets, geo_part, col_part)

    initial = jnp.zeros((columns.shape[0], targets.shape[1]), jnp.float32)
    return lax.fori_loop(0, block_count, add_block, initial)


def per_device(filament_slot, wire_radius, strand_radius, test_matrix):
    targets = filament_geometry(filament_slot, wire_radius, strand_radius)
    geo_row, col_row = (
        lax.all_gather(targets, ("col", "sub"), axis=1, tiled=True),
        lax.all_gather(test_matrix, ("col", "sub"), axis=1, tiled=True),
    )
    sketch = sweep_sources(targets, geo_row, col_row)
    half_cycle = lax.axis_size("row") // 2

    def both_ways(turn_index, state_now):
        running, ahead_geo, ahead_cols, behind_geo, behind_cols = state_now
        ahead_geo, ahead_cols = from_behind((ahead_geo, ahead_cols), "row", 1)
        behind_geo, behind_cols = from_behind((behind_geo, behind_cols), "row", -1)
        running = running + sweep_sources(targets, ahead_geo, ahead_cols)
        running = running + sweep_sources(targets, behind_geo, behind_cols)
        return (running, ahead_geo, ahead_cols, behind_geo, behind_cols)

    state_end = lax.fori_loop(
        1, half_cycle, both_ways, (sketch, geo_row, col_row, geo_row, col_row)
    )
    far_geo, far_cols = from_behind((state_end[1], state_end[2]), "row", 1)
    sketch = state_end[0] + sweep_sources(targets, far_geo, far_cols)
    local_gram = jnp.dot(
        sketch, sketch.T, precision=lax.Precision.HIGHEST, preferred_element_type=jnp.float32
    )
    gram_matrix = lax.psum(local_gram, ("row", "col", "sub"))
    cholesky_low = jnp.linalg.cholesky(gram_matrix)
    solved = jax.scipy.linalg.solve_triangular(cholesky_low, sketch, lower=True)
    filament_total = (
        sketch.shape[1] * lax.axis_size("row") * lax.axis_size("col") * lax.axis_size("sub")
    )
    scale_root = math.sqrt(filament_total)
    return (solved * scale_root, cholesky_low.T / scale_root)


def solution(mesh):
    return jax.shard_map(
        per_device,
        mesh=mesh,
        in_specs=(
            P(("grp", "row", "col", "sub")),
            P(("grp", "row", "col", "sub")),
            P("grp"),
            P(None, ("grp", "row", "col", "sub")),
        ),
        out_specs=(P(None, ("grp", "row", "col", "sub")), P("grp", None)),
        check_vma=False,
    )
```

profile of v0, /device:TPU:0, one launch (start us, length us, event | category | flops | bytes accessed | tf_op | source)
XLA Modules:
  0.0 137.8 jit_solution(15863045663286231874)
XLA Ops:
  0.6 0.0 copy-start.1
  0.6 0.0 copy-start
  0.7 0.0 copy-start.2
  0.7 9.0 %all_gather.7 = f32[64,2048]{1,0:T(8,128)S(1)} all-gather(f32[64,512]{1,0:T(8,128)} %param.7), channel_id=1, replica_groups=mesh['grp'=2,'row'=4,'col'=2,'sub'=2] {'col','sub'}, dimensions={1}, use_global_device_ids=true | all-gather | bytes 655360 | tf_op jit(solution)/shard_map/all_gather | solution.py:89
  9.6 3.6 %collective-permute-start.3 = (f32[64,2048]{1,0:T(8,128)S(1)}, f32[64,2048]{1,0:T(8,128)S(1)}, u32[]{:S(2)}, u32[]{:S(2)}) collective-permute-start(f32[64,2048]{1,0:T(8,128)S(1)} %all_gather.7), channel_id=1, source_target_pairs={{0,12},{4,0},{8,4},{12,8},{1,13},{5,1},{9,5},{13,9},{2,14},{6,2},{... | collective-permute-start | bytes 1572872 | tf_op jit(solution)/shard_map/while/body/eval_jaxpr/ppermute | solution.py:17
  13.2 0.0 collective-permute-start.1
  13.2 0.0 copy-done.1
  13.2 0.1 fusion.146
  13.3 0.0 copy-done
  13.3 0.0 copy-done.2
  13.3 0.1 select_reduce_fusion
  13.5 5.2 %all_gather.6 = f32[7,2048]{1,0:T(8,128)S(1)} all-gather(f32[7,512]{1,0:T(8,128)S(1)} %stack.27), channel_id=1, replica_groups=mesh['grp'=2,'row'=4,'col'=2,'sub'=2] {'col','sub'}, dimensions={1}, use_global_device_ids=true | all-gather | bytes 71680 | tf_op jit(solution)/shard_map/all_gather | solution.py:88
  18.8 3.8 %collective-permute-start.2 = (f32[7,2048]{1,0:T(8,128)S(1)}, f32[7,2048]{1,0:T(8,128)S(1)}, u32[]{:S(2)}, u32[]{:S(2)}) collective-permute-start(f32[7,2048]{1,0:T(8,128)S(1)} %all_gather.6), channel_id=1, source_target_pairs={{0,12},{4,0},{8,4},{12,8},{1,13},{5,1},{9,5},{13,9},{2,14},{6,2},{... | collective-permute-start | bytes 172040 | tf_op jit(solution)/shard_map/while/body/eval_jaxpr/ppermute | solution.py:17
  22.6 0.0 collective-permute-start
  22.6 5.4 %fusion.54 = f32[512,64]{0,1:T(8,128)S(1)} fusion(f32[64,2048]{1,0:T(8,128)S(1)} %all_gather.7, f32[512]{0:T(512)S(1)} %mul.293, f32[2048]{0:T(1024)S(1)} %bitcast.74, f32[512]{0:T(512)S(1)} %get-tuple-element.81, f32[2048]{0:T(1024)S(1)} %bitcast.75, f32[512]{0:T(512)S(1)} %get-tuple-element.79, f32[2048]{0:T(1024)S(1)} %bitcast.76, ...), kind=kOutput, calls=%fused_computation.54 | convolution fusion | flops 822083584 | bytes 724992 | tf_op jit(solution)/shard_map/dot_general | solution.py:63
  28.0 11.9 %collective-permute-done = f32[7,2048]{1,0:T(8,128)S(1)} collective-permute-done((f32[7,2048]{1,0:T(8,128)S(1)}, f32[7,2048]{1,0:T(8,128)S(1)}, u32[]{:S(2)}, u32[]{:S(2)}) %collective-permute-start) | collective-permute-done | bytes 57376 | tf_op jit(solution)/shard_map/while/body/eval_jaxpr/ppermute | solution.py:17
  40.0 1.6 %collective-permute-start.4 = (f32[7,2048]{1,0:T(8,128)S(1)}, f32[7,2048]{1,0:T(8,128)S(1)}, u32[]{:S(2)}, u32[]{:S(2)}) collective-permute-start(f32[7,2048]{1,0:T(8,128)S(1)} %collective-permute-done), channel_id=1, source_target_pairs={{0,4},{4,8},{8,12},{12,0},{1,5},{5,9},{9,13},{13,1},{2,6},{6,10},{... | collective-permute-start | bytes 172040 | tf_op jit(solution)/shard_map/ppermute | solution.py:17
  41.6 0.0 collective-permute-done.2
  41.6 4.4 %collective-permute-done.4 = f32[7,2048]{1,0:T(8,128)S(1)} collective-permute-done((f32[7,2048]{1,0:T(8,128)S(1)}, f32[7,2048]{1,0:T(8,128)S(1)}, u32[]{:S(2)}, u32[]{:S(2)}) %collective-permute-start.4) | collective-permute-done | bytes 57376 | tf_op jit(solution)/shard_map/ppermute | solution.py:17
  46.1 0.0 collective-permute-done.1
  46.1 0.2 collective-permute-start.5
  46.4 0.0 collective-permute-done.3
  46.4 5.5 %fusion.18 = f32[512,64]{0,1:T(8,128)S(1)} fusion(f32[64,2048]{1,0:T(8,128)S(1)} %collective-permute-done.3, f32[2048]{0:T(1024)S(1)} %bitcast.67, f32[2048]{0:T(1024)S(1)} %bitcast.68, f32[2048]{0:T(1024)S(1)} %bitcast.69, f32[2048]{0:T(1024)S(1)} %bitcast.70, f32[2048]{0:T(1024)S(1)} %bitcast.71, f32[2048]{0:T(1024)S(1)} %bitcast.72, ...), kind=kOutput, calls=%fused_computation.18 | convolution fusion | flops 822083584 | bytes 724992 | tf_op jit(solution)/shard_map/while/body/eval_jaxpr/dot_general | solution.py:63
  51.9 5.5 %fusion.131 = f32[512,64]{0,1:T(8,128)S(1)} fusion(f32[512,64]{0,1:T(8,128)S(1)} %fusion.18, f32[512,64]{0,1:T(8,128)S(1)} %fusion.54, f32[64,2048]{1,0:T(8,128)S(1)} %collective-permute-done.1, f32[2048]{0:T(1024)S(1)} %bitcast.53, f32[2048]{0:T(1024)S(1)} %bitcast.54, f32[2048]{0:T(1024)S(1)} %bitcast.55, f32[2048]{0:T(1024)S(1)} %bitcast.56, ...), kind=kOutput, calls=%fused_computation.130 | convolution fusion | flops 822149120 | bytes 987136 | tf_op jit(solution)/shard_map/while/body/eval_jaxpr/dot_general | solution.py:63
  57.3 3.1 %collective-permute-done.5 = f32[64,2048]{1,0:T(8,128)S(1)} collective-permute-done((f32[64,2048]{1,0:T(8,128)S(1)}, f32[64,2048]{1,0:T(8,128)S(1)}, u32[]{:S(2)}, u32[]{:S(2)}) %collective-permute-start.5) | collective-permute-done | bytes 524320 | tf_op jit(solution)/shard_map/ppermute | solution.py:17
  60.4 5.7 %fusion.134 = f32[512,64]{0,1:T(8,128)S(1)} fusion(f32[512,64]{0,1:T(8,128)S(1)} %fusion.131, f32[64,2048]{1,0:T(8,128)S(1)} %collective-permute-done.5, f32[2048]{0:T(1024)S(1)} %bitcast.60, f32[2048]{0:T(1024)S(1)} %bitcast.61, f32[2048]{0:T(1024)S(1)} %bitcast.62, f32[2048]{0:T(1024)S(1)} %bitcast.63, f32[2048]{0:T(1024)S(1)} %bitcast.64, ...), kind=kOutput, calls=%fused_computation.131 | convolution fusion | flops 822116352 | bytes 856064 | tf_op jit(solution)/shard_map/dot_general | solution.py:63
  66.1 0.3 fusion.151
  66.3 57.7 %psum.7 = f32[64,64]{0,1:T(8,128)S(1)} all-reduce(f32[64,64]{0,1:T(8,128)S(1)} %fusion.151), channel_id=1, replica_groups=mesh['grp'=2,'row'=4,'col'=2,'sub'=2] {'row','col','sub'}, use_global_device_ids=true, to_apply=%region_1.2 | all-reduce | flops 4096 | bytes 32768 | tf_op jit(solution)/shard_map/psum | solution.py:110
  124.0 0.1 copy.10
  124.1 5.8 %cholesky.16 = f32[64,64]{1,0:T(8,128)S(1)} custom-call(f32[64,64]{1,0:T(8,128)S(1)} %fusion.138), custom_call_target="Cholesky" | custom-call | tf_op jit(solution)/shard_map/jit(cholesky)/cholesky | solution.py:111
  129.9 0.6 compare_reduce_fusion
  130.6 0.7 multiply_bitcast_fusion
  131.3 4.9 %custom-call.7 = f32[1,64,64]{1,2,0:T(8,128)S(1)} custom-call(f32[1,64,64]{2,1,0:T(8,128)S(1)} %get-tuple-element.74), custom_call_target="InvertDiagBlocksLowerTriangular" | custom-call | tf_op jit(solution)/shard_map/jit(_solve_triangular)/triangular_solve | solution.py:112
  136.2 1.0 convolution_multiply_fusion
  137.1 0.7 copy.11
  (10 shorter events, 0.3 us)
Async XLA Ops:
  0.6 12.6 %copy-start.1 = (s32[512]{0:T(512)S(1)}, s32[512]{0:T(512)}, u32[]{:S(2)}) copy-start(s32[512]{0:T(512)} %param.4) | copy-start | bytes 6148
  0.6 12.6 %copy-start = (f32[512]{0:T(512)S(1)}, f32[512]{0:T(512)}, u32[]{:S(2)}) copy-start(f32[512]{0:T(512)} %param.5) | copy-start | bytes 6148
  0.7 12.7 %copy-start.2 = (f32[64]{0:T(128)S(1)}, f32[64]{0:T(128)}, u32[]{:S(2)}) copy-start(f32[64]{0:T(128)} %param.6) | copy-start | bytes 772
  9.6 36.8 %collective-permute-start.3 = (f32[64,2048]{1,0:T(8,128)S(1)}, f32[64,2048]{1,0:T(8,128)S(1)}, u32[]{:S(2)}, u32[]{:S(2)}) collective-permute-start(f32[64,2048]{1,0:T(8,128)S(1)} %all_gather.7), channel_id=1, source_target_pairs={{0,12},{4,0},{8,4},{12,8},{1,13},{5,1},{9,5},{13,9},{2,14},{6,2},{... | collective-permute-start | bytes 1572872 | tf_op jit(solution)/shard_map/while/body/eval_jaxpr/ppermute | solution.py:17
  13.2 32.9 %collective-permute-start.1 = (f32[64,2048]{1,0:T(8,128)S(1)}, f32[64,2048]{1,0:T(8,128)S(1)}, u32[]{:S(2)}, u32[]{:S(2)}) collective-permute-start(f32[64,2048]{1,0:T(8,128)S(1)} %all_gather.7), channel_id=1, source_target_pairs={{0,4},{4,8},{8,12},{12,0},{1,5},{5,9},{9,13},{13,1},{2,6},{6,10},{... | collective-permute-start | bytes 1572872 | tf_op jit(solution)/shard_map/while/body/eval_jaxpr/ppermute | solution.py:17
  18.8 22.8 %collective-permute-start.2 = (f32[7,2048]{1,0:T(8,128)S(1)}, f32[7,2048]{1,0:T(8,128)S(1)}, u32[]{:S(2)}, u32[]{:S(2)}) collective-permute-start(f32[7,2048]{1,0:T(8,128)S(1)} %all_gather.6), channel_id=1, source_target_pairs={{0,12},{4,0},{8,4},{12,8},{1,13},{5,1},{9,5},{13,9},{2,14},{6,2},{... | collective-permute-start | bytes 172040 | tf_op jit(solution)/shard_map/while/body/eval_jaxpr/ppermute | solution.py:17
  22.6 17.3 %collective-permute-start = (f32[7,2048]{1,0:T(8,128)S(1)}, f32[7,2048]{1,0:T(8,128)S(1)}, u32[]{:S(2)}, u32[]{:S(2)}) collective-permute-start(f32[7,2048]{1,0:T(8,128)S(1)} %all_gather.6), channel_id=1, source_target_pairs={{0,4},{4,8},{8,12},{12,0},{1,5},{5,9},{9,13},{13,1},{2,6},{6,10},{... | collective-permute-start | bytes 172040 | tf_op jit(solution)/shard_map/while/body/eval_jaxpr/ppermute | solution.py:17
  40.0 6.1 %collective-permute-start.4 = (f32[7,2048]{1,0:T(8,128)S(1)}, f32[7,2048]{1,0:T(8,128)S(1)}, u32[]{:S(2)}, u32[]{:S(2)}) collective-permute-start(f32[7,2048]{1,0:T(8,128)S(1)} %collective-permute-done), channel_id=1, source_target_pairs={{0,4},{4,8},{8,12},{12,0},{1,5},{5,9},{9,13},{13,1},{2,6},{6,10},{... | collective-permute-start | bytes 172040 | tf_op jit(solution)/shard_map/ppermute | solution.py:17
  46.1 14.3 %collective-permute-start.5 = (f32[64,2048]{1,0:T(8,128)S(1)}, f32[64,2048]{1,0:T(8,128)S(1)}, u32[]{:S(2)}, u32[]{:S(2)}) collective-permute-start(f32[64,2048]{1,0:T(8,128)S(1)} %collective-permute-done.1), channel_id=1, source_target_pairs={{0,4},{4,8},{8,12},{12,0},{1,5},{5,9},{9,13},{13,1},{2,6},{6,10},{... | collective-permute-start | bytes 1572872 | tf_op jit(solution)/shard_map/ppermute | solution.py:17
where the time goes:
time: 138 us
  blocking collectives  71.9 us (52%)
  matrix products  23.2 us (17%)
  waiting for transfers between devices  19.4 us (14%)
  other arithmetic  12.3 us (9%)
  starting transfers between devices  9.3 us (7%)
    psum x1, blocking collectives, per_device(): gram_matrix = lax.psum(local_gram, ('row', 'col', 'sub'))  57.7 us
    dot_general x4, matrix products, source_block(): jnp.dot(columns, kernel, precision=lax.Precision.HIGHEST, preferred_eleme...  22 us
    ppermute x6, waiting for transfers between devices, from_behind(): lax.ppermute(shard, axis, [(i, (i + by) % count) for i in range(count)])  19.4 us
    ppermute x6, starting transfers between devices, from_behind(): lax.ppermute(shard, axis, [(i, (i + by) % count) for i in range(count)])  9.3 us
    all_gather x1, blocking collectives, per_device(): lax.all_gather(test_matrix, ('col', 'sub'), axis=1, tiled=True)  8.96 us
    another operation x3, other arithmetic, per_device(): cholesky_low = jnp.linalg.cholesky(gram_matrix)  6.52 us
    all_gather x1, blocking collectives, per_device(): lax.all_gather(targets, ('col', 'sub'), axis=1, tiled=True)  5.25 us
    another operation x1, other arithmetic, per_device(): solved = jax.scipy.linalg.solve_triangular(cholesky_low, sketch, lower=True)  4.9 us
  transfers between devices with their start and end apart: 6, of which 3 were waited for; matrix products, arithmetic and copies ran while one was open for 12% of the time, Pallas kernels for 0%

commit v1 on v0

v1 whole, which is shorter than its diff:
```python
import functools
import math

import jax
import jax.numpy as jnp
from jax import lax
from jax.experimental import pallas as pl
from jax.experimental.pallas import tpu as pltpu
from jax.sharding import PartitionSpec as P

SEGMENTS = 128
GEO_ROWS = 8
MU_SCALE = 1e-05
TWIST_RATE = 4.0 * math.pi
FOLDED = MU_SCALE * TWIST_RATE * TWIST_RATE / 2.0
OFFSET = 2.0 / (TWIST_RATE * TWIST_RATE)
MESH = pl.DeviceIdType.MESH


def local_geometry(slot, wire, strand_radius):
    strand = slot // SEGMENTS
    segment = slot % SEGMENTS
    strand_count = strand_radius.shape[1]
    count = slot.shape[1]
    onehot = (
        lax.broadcasted_iota(jnp.int32, (strand_count, count), 0) == strand
    ).astype(jnp.float32)
    radius = jnp.dot(
        jnp.broadcast_to(strand_radius, (8, strand_count)),
        onehot,
        precision=lax.Precision.HIGHEST,
        preferred_element_type=jnp.float32,
    )[0:1]
    height = (segment.astype(jnp.float32) + 0.5) / SEGMENTS
    angle = 2.0 * math.pi / strand_count * strand.astype(jnp.float32) + TWIST_RATE * height
    root = math.sqrt(2.0)
    x = root * radius * jnp.cos(angle)
    y = root * radius * jnp.sin(angle)
    z = root * (height - 0.5)
    e = 0.5 * (x * x + y * y + z * z) + wire * wire
    return jnp.concatenate([x, y, z, e, x, y, z, e], axis=0)


def sketch_kernel(
    dims, slot_ref, wire_ref, radius_ref, test_ref, sketch_ref, gram_ref,
    pay, tgeo, columns, halves, partial, landed, gram_plane, gram_line,
    pay_send, pay_recv, geo_send, geo_recv, sum_send, sum_recv,
    gp_send, gp_recv, gl_send, gl_recv,
):
    rows, cols, subs = dims
    plane = cols * subs
    rank, count = test_ref.shape
    row, col, sub = lax.axis_index("row"), lax.axis_index("col"), lax.axis_index("sub")

    def plane_peer(o):
        return {
            "col": lax.rem(col + o // subs, cols),
            "sub": lax.rem(sub + o % subs, subs),
        }

    def opposite(o):
        return (cols - o // subs) % cols * subs + (subs - o % subs) % subs

    def line_peer(k):
        return {"row": lax.rem(row + k, rows)}

    barrier = pltpu.get_barrier_semaphore()
    for o in range(1, plane):
        pl.semaphore_signal(barrier, inc=1, device_id=plane_peer(o), device_id_type=MESH)
    for k in range(1, rows):
        pl.semaphore_signal(barrier, inc=1, device_id=line_peer(k), device_id_type=MESH)

    geo = local_geometry(slot_ref[...], wire_ref[...], radius_ref[...])
    pay[0, :rank, :] = test_ref[...]
    pay[0, rank:, :] = geo
    tgeo[0] = geo
    pl.semaphore_wait(barrier, plane + rows - 2)

    def copy_geo(o):
        return pltpu.make_async_remote_copy(
            src_ref=pay.at[0, pl.ds(rank, GEO_ROWS)], dst_ref=tgeo.at[opposite(o)],
            send_sem=geo_send.at[o], recv_sem=geo_recv.at[opposite(o)],
            device_id=plane_peer(o), device_id_type=MESH,
        )

    def copy_pay(k):
        return pltpu.make_async_remote_copy(
            src_ref=pay.at[0], dst_ref=pay.at[k],
            send_sem=pay_send.at[k], recv_sem=pay_recv.at[k],
            device_id=line_peer(k), device_id_type=MESH,
        )

    def copy_sum(o):
        return pltpu.make_async_remote_copy(
            src_ref=partial.at[o], dst_ref=landed.at[o],
            send_sem=sum_send.at[o], recv_sem=sum_recv.at[o],
            device_id=plane_peer(o), device_id_type=MESH,
        )

    def order(index):
        return (index + 1) // 2 if index % 2 else (rows - index // 2) % rows

    for o in reversed(range(1, plane)):
        copy_geo(o).start()
    for index in range(1, rows):
        copy_pay(order(index)).start()

    def prepare(k):
        columns[...] = jnp.concatenate(
            [pay[k, rank:, :]] * (128 // GEO_ROWS), axis=0
        ).T
        test = pay[k, :rank, :]
        high = test.astype(jnp.bfloat16)
        halves[:rank, :] = high
        halves[rank:, :] = (test - high.astype(jnp.float32)).astype(jnp.bfloat16)

    def block(o, first):
        xs, ys = columns[:, 0:1], columns[:, 1:2]
        zs, es = columns[:, 2:3], columns[:, 3:4]
        xt, yt = tgeo[o, 0:1, :], tgeo[o, 1:2, :]
        zt, et = tgeo[o, 2:3, :], tgeo[o, 3:4, :]
        cross = xs * xt + ys * yt
        distance = (es + et) - cross - zs * zt
        kernel = (cross + OFFSET) * lax.rsqrt(distance)
        high = kernel.astype(jnp.bfloat16)
        low = (kernel - high.astype(jnp.float32)).astype(jnp.bfloat16)
        both = jnp.dot(halves[...], high, preferred_element_type=jnp.float32)
        rest = jnp.dot(halves[:rank, :], low, preferred_element_type=jnp.float32)
        term = both[:rank] + (both[rank:] + rest)
        if first:
            partial[o] = term
        else:
            partial[o] += term

    prepare(0)
    block(0, True)
    for o in range(1, plane):
        copy_geo(opposite(o)).wait_recv()

    @pl.loop(1, plane)
    def _(o):
        block(o, True)

    for index in range(1, rows - 1):
        copy_pay(order(index)).wait_recv()
        prepare(order(index))

        @pl.loop(0, plane)
        def _(o):
            block(o, False)

    copy_pay(order(rows - 1)).wait_recv()
    prepare(order(rows - 1))
    for o in reversed(range(1, plane)):
        block(o, False)
        copy_sum(o).start()
    block(0, False)
    sketch = partial[0]
    for o in range(1, plane):
        copy_sum(o).wait_recv()
        sketch = sketch + landed[o]
    sketch_ref[...] = sketch

    gram = lax.dot_general(
        sketch, sketch, (((1,), (1,)), ((), ())),
        precision=lax.Precision.HIGHEST, preferred_element_type=jnp.float32,
    )
    place = col * subs + sub
    gram_plane[place] = gram

    def copy_gp(o):
        return pltpu.make_async_remote_copy(
            src_ref=gram_plane.at[place], dst_ref=gram_plane.at[place],
            send_sem=gp_send.at[o], recv_sem=gp_recv.at[o],
            device_id=plane_peer(o), device_id_type=MESH,
        )

    def copy_gl(k):
        return pltpu.make_async_remote_copy(
            src_ref=gram_line.at[row], dst_ref=gram_line.at[row],
            send_sem=gl_send.at[k], recv_sem=gl_recv.at[k],
            device_id=line_peer(k), device_id_type=MESH,
        )

    for o in range(1, plane):
        copy_gp(o).start()
    for o in range(1, plane):
        copy_gp(o).wait()
    total = gram_plane[0]
    for o in range(1, plane):
        total = total + gram_plane[o]
    gram_line[row] = total
    for k in range(1, rows):
        copy_gl(k).start()
    for k in range(1, rows):
        copy_gl(k).wait()
    total = gram_line[0]
    for k in range(1, rows):
        total = total + gram_line[k]
    gram_ref[...] = total

    for o in range(1, plane):
        copy_geo(o).wait_send()
        copy_sum(o).wait_send()
    for k in range(1, rows):
        copy_pay(k).wait_send()


def factor_kernel(scale, sketch_ref, gram_ref, basis_ref, factor_ref):
    rank = gram_ref.shape[0]
    tiles = rank // 8
    eye = (
        lax.broadcasted_iota(jnp.int32, (rank, rank), 0)
        == lax.broadcasted_iota(jnp.int32, (rank, rank), 1)
    ).astype(jnp.float32)
    wide = jnp.concatenate([gram_ref[...], eye], axis=1)
    parts = [wide[8 * t : 8 * t + 8] for t in range(tiles)]
    place = lax.broadcasted_iota(jnp.int32, (8, 2 * rank), 0)
    for j in range(rank):
        own, line = divmod(j, 8)
        pivot_row = parts[own][line : line + 1]
        scaled = pivot_row * (1.0 / pivot_row[:, j : j + 1])
        for t in range(own, tiles):
            update = parts[t][:, j : j + 1] * scaled
            if t == own:
                update = jnp.where(place > line, update, 0.0)
            parts[t] = parts[t] - update
    wide = jnp.concatenate(parts, axis=0)
    pivots = jnp.sum(wide[:, :rank] * eye, axis=1, keepdims=True)
    wide = wide * lax.rsqrt(pivots)
    upper = (
        lax.broadcasted_iota(jnp.int32, (rank, rank), 0)
        <= lax.broadcasted_iota(jnp.int32, (rank, rank), 1)
    )
    factor_ref[...] = jnp.where(upper, wide[:, :rank], 0.0) * (FOLDED / scale)
    basis_ref[...] = jnp.dot(
        wide[:, rank:] * scale, sketch_ref[...],
        precision=lax.Precision.HIGHEST, preferred_element_type=jnp.float32,
    )


def per_device(filament_slot, wire_radius, strand_radius, test_matrix):
    dims = tuple(lax.axis_size(name) for name in ("row", "col", "sub"))
    rows, plane = dims[0], dims[1] * dims[2]
    rank, count = test_matrix.shape
    vmem = pl.BlockSpec(memory_space=pltpu.VMEM)
    f32 = jnp.float32
    dma = pltpu.SemaphoreType.DMA
    sketch, gram = pl.pallas_call(
        functools.partial(sketch_kernel, dims),
        out_shape=(
            jax.ShapeDtypeStruct((rank, count), f32),
            jax.ShapeDtypeStruct((rank, rank), f32),
        ),
        in_specs=[vmem] * 4,
        out_specs=(vmem, vmem),
        scratch_shapes=[
            pltpu.VMEM((rows, rank + GEO_ROWS, count), f32),
            pltpu.VMEM((plane, GEO_ROWS, count), f32),
            pltpu.VMEM((count, 128), f32),
            pltpu.VMEM((2 * rank, count), jnp.bfloat16),
            pltpu.VMEM((plane, rank, count), f32),
            pltpu.VMEM((plane, rank, count), f32),
            pltpu.VMEM((plane, rank, rank), f32),
            pltpu.VMEM((rows, rank, rank), f32),
            dma((rows,)), dma((rows,)), dma((plane,)), dma((plane,)), dma((plane,)), dma((plane,)),
            dma((plane,)), dma((plane,)), dma((rows,)), dma((rows,)),
        ],
        compiler_params=pltpu.CompilerParams(
            collective_id=0, has_side_effects=True, vmem_limit_bytes=48 * 1024 * 1024
        ),
    )(
        filament_slot.reshape(1, count),
        wire_radius.reshape(1, count),
        strand_radius.reshape(1, -1),
        test_matrix,
    )
    scale = math.sqrt(count * rows * plane)
    return pl.pallas_call(
        functools.partial(factor_kernel, scale),
        out_shape=(
            jax.ShapeDtypeStruct((rank, count), f32),
            jax.ShapeDtypeStruct((rank, rank), f32),
        ),
        in_specs=[vmem] * 2,
        out_specs=(vmem, vmem),
        compiler_params=pltpu.CompilerParams(vmem_limit_bytes=16 * 1024 * 1024),
    )(sketch, gram)


def solution(mesh):
    return jax.shard_map(
        per_device,
        mesh=mesh,
        in_specs=(
            P(("grp", "row", "col", "sub")),
            P(("grp", "row", "col", "sub")),
            P("grp"),
            P(None, ("grp", "row", "col", "sub")),
        ),
        out_specs=(P(None, ("grp", "row", "col", "sub")), P("grp", None)),
        check_vma=False,
    )
```

time: 138 us -> 45.5 us (0.33)
  blocking collectives: 71.9 us -> 0 us
  Pallas kernels: 0 us -> 43.1 us
  matrix products: 23.2 us -> 0 us
  waiting for transfers between devices: 19.4 us -> 0 us
  other arithmetic: 12.3 us -> 0 us
  starting transfers between devices: 9.3 us -> 0 us
    psum x1 -> x0, blocking collectives: 57.7 us -> none  [per_device(): gram_matrix = lax.psum(local_gram, ('row', 'col', 'sub'))]
    pallas_call x0 -> x2, Pallas kernels: none -> 43.1 us  [the longest x1 36.7 us: per_device(): pl.pallas_call(functools.partial(sketch_kernel, dims), out_shape=(jax.Sha...]
    dot_general x5 -> x0, matrix products: 22.3 us -> none  [the longest x4 22 us: source_block(): jnp.dot(columns, kernel, precision=lax.Precision.HIGHEST, preferred_eleme...]
    ppermute x6 -> x0, waiting for transfers between devices: 19.4 us -> none  [from_behind(): lax.ppermute(shard, axis, [(i, (i + by) % count) for i in range(count)])]
    all_gather x2 -> x0, blocking collectives: 14.2 us -> none  [the longest x1 8.96 us: per_device(): lax.all_gather(test_matrix, ('col', 'sub'), axis=1, tiled=True)]
    another operation x4 -> x0, other arithmetic: 11.4 us -> none  [the longest x3 6.52 us: per_device(): cholesky_low = jnp.linalg.cholesky(gram_matrix)]
    ppermute x6 -> x0, starting transfers between devices: 9.3 us -> none  [from_behind(): lax.ppermute(shard, axis, [(i, (i + by) % count) for i in range(count)])]
  transfers between devices with their start and end apart: 6 -> 0, of which waited for: 3 -> 0; matrix products, arithmetic and copies ran while one was open for 12% -> 0% of each run, Pallas kernels for 0% -> 0%
where the time goes in v1:
time: 45.5 us; the launch traced here: 45.3 us
  Pallas kernels  43.1 us (95%)
  local copies, waits for them, and re-layouts  1.58 us (3%)
  between operations  0.66 us (1%)
    pallas_call x1, Pallas kernels, per_device(): pl.pallas_call(functools.partial(sketch_kernel, dims), out_shape=(jax.Sha...  36.7 us
    pallas_call x1, Pallas kernels, per_device(): pl.pallas_call(functools.partial(factor_kernel, scale), out_shape=(jax.Sh...  6.41 us
    unnamed x8, local copies, waits for them, and re-layouts  1.58 us

profile of v1, /device:TPU:0, one launch (start us, length us, event | category | flops | bytes accessed | tf_op | source)
XLA Modules:
  0.0 45.3 jit_solution(15385030433512760277)
XLA Ops:
  0.6 0.0 copy-start.2
  0.6 0.0 copy-start.1
  0.7 0.0 copy-start.3
  0.7 0.7 %copy-done.2 = f32[512]{0:T(512)S(1)} copy-done((f32[512]{0:T(512)S(1)}, f32[512]{0:T(512)}, u32[]{:S(2)}) %copy-start.2) | copy-done | bytes 2072
  1.3 0.0 copy-done.1
  1.3 0.0 copy-done.3
  1.3 0.0 copy-start
  1.3 0.9 %copy-done = f32[64,512]{1,0:T(8,128)S(1)} copy-done((f32[64,512]{1,0:T(8,128)S(1)}, f32[64,512]{1,0:T(8,128)}, u32[]{:S(2)}) %copy-start) | copy-done | bytes 131096
  2.2 36.7 %shard_map.59 = (f32[64,512]{1,0:T(8,128)S(1)}, f32[64,64]{1,0:T(8,128)S(1)}) custom-call(s32[1,512]{1,0:T(1,128)S(1)} %bitcast.3, f32[1,512]{1,0:T(1,128)S(1)} %bitcast.4, f32[1,64]{1,0:T(1,128)S(1)} %bitcast.5, f32[64,512]{1,0:T(8,128)S(1)} %copy-done), custom_call_target="tpu_custom_call" | custom-call | tf_op jit(solution)/shard_map/pallas_call | solution.py:249
  38.9 6.4 %shard_map.60 = (f32[64,512]{1,0:T(8,128)}, f32[64,64]{1,0:T(8,128)}) custom-call(f32[64,512]{1,0:T(8,128)S(1)} %get-tuple-element.4.sketch_ref, f32[64,64]{1,0:T(8,128)S(1)} %get-tuple-element.5.gram_ref), custom_call_target="tpu_custom_call" | custom-call | tf_op jit(solution)/shard_map/pallas_call | solution.py:279
Async XLA Ops:
  0.6 0.7 %copy-start.2 = (f32[512]{0:T(512)S(1)}, f32[512]{0:T(512)}, u32[]{:S(2)}) copy-start(f32[512]{0:T(512)} %param.5) | copy-start | bytes 6148
  0.6 0.7 %copy-start.1 = (s32[512]{0:T(512)S(1)}, s32[512]{0:T(512)}, u32[]{:S(2)}) copy-start(s32[512]{0:T(512)} %param.4) | copy-start | bytes 6148
  0.7 0.7 %copy-start.3 = (f32[64]{0:T(128)S(1)}, f32[64]{0:T(128)}, u32[]{:S(2)}) copy-start(f32[64]{0:T(128)} %param.6) | copy-start | bytes 772
  1.3 0.9 %copy-start = (f32[64,512]{1,0:T(8,128)S(1)}, f32[64,512]{1,0:T(8,128)}, u32[]{:S(2)}) copy-start(f32[64,512]{1,0:T(8,128)} %test_ref.1) | copy-start | bytes 393220

commit v2 on v1

v2 whole, which is shorter than its diff:
```python
import functools
import math

import jax
import jax.numpy as jnp
from jax import lax
from jax.experimental import pallas as pl
from jax.experimental.pallas import tpu as pltpu
from jax.sharding import PartitionSpec as P

SEGMENTS = 128
GEO_ROWS = 8
MU_SCALE = 1e-05
TWIST_RATE = 4.0 * math.pi
FOLDED = MU_SCALE * TWIST_RATE * TWIST_RATE / 2.0
OFFSET = 2.0 / (TWIST_RATE * TWIST_RATE)
MESH = pl.DeviceIdType.MESH


def local_geometry(slot, wire, strand_radius):
    strand = slot // SEGMENTS
    segment = slot % SEGMENTS
    strand_count = strand_radius.shape[1]
    count = slot.shape[1]
    onehot = (
        lax.broadcasted_iota(jnp.int32, (strand_count, count), 0) == strand
    ).astype(jnp.float32)
    radius = jnp.dot(
        jnp.broadcast_to(strand_radius, (8, strand_count)),
        onehot,
        precision=lax.Precision.HIGHEST,
        preferred_element_type=jnp.float32,
    )[0:1]
    height = (segment.astype(jnp.float32) + 0.5) / SEGMENTS
    angle = 2.0 * math.pi / strand_count * strand.astype(jnp.float32) + TWIST_RATE * height
    root = math.sqrt(2.0)
    x = root * radius * jnp.cos(angle)
    y = root * radius * jnp.sin(angle)
    z = root * (height - 0.5)
    e = 0.5 * (x * x + y * y + z * z) + wire * wire
    return jnp.concatenate([x, y, z, e, x, y, z, e], axis=0)


def sketch_kernel(
    dims, slot_hbm, wire_hbm, radius_hbm, test_hbm, sketch_ref, gram_ref,
    slot_ref, wire_ref, radius_ref,
    pay, tgeo, columns, halves, partial, landed, gram_plane, gram_line, load_sem,
    pay_send, pay_recv, fwd_send, fwd_recv, geo_send, geo_recv, sum_send, sum_recv,
    gp_send, gp_recv, gl_send, gl_recv,
):
    rows, cols, subs = dims
    plane = cols * subs
    rank, count = test_hbm.shape
    row, col, sub = lax.axis_index("row"), lax.axis_index("col"), lax.axis_index("sub")

    def plane_peer(o):
        return {
            "col": lax.rem(col + o // subs, cols),
            "sub": lax.rem(sub + o % subs, subs),
        }

    def line_peer(k):
        return {"row": lax.rem(row + k, rows)}

    def col_peer(o):
        return {"col": lax.rem(col + o, cols)}

    loads = [
        pltpu.make_async_copy(slot_hbm, slot_ref, load_sem.at[0]),
        pltpu.make_async_copy(wire_hbm, wire_ref, load_sem.at[1]),
        pltpu.make_async_copy(radius_hbm, radius_ref, load_sem.at[2]),
        pltpu.make_async_copy(test_hbm, pay.at[0, 0, pl.ds(0, rank)], load_sem.at[3]),
    ]
    for load in loads:
        load.start()
    barrier = pltpu.get_barrier_semaphore()
    for o in range(1, plane):
        pl.semaphore_signal(barrier, inc=1, device_id=plane_peer(o), device_id_type=MESH)
    for k in range(1, rows):
        pl.semaphore_signal(barrier, inc=1, device_id=line_peer(k), device_id_type=MESH)

    for load in loads[:3]:
        load.wait()
    geo = local_geometry(slot_ref[...], wire_ref[...], radius_ref[...])
    pay[0, 0, rank:, :] = geo
    tgeo[0] = geo
    partial[...] = jnp.zeros_like(partial)
    loads[3].wait()
    pl.semaphore_wait(barrier, plane + rows - 2)

    def copy_geo(o):
        return pltpu.make_async_remote_copy(
            src_ref=pay.at[0, 0, pl.ds(rank, GEO_ROWS)], dst_ref=tgeo.at[cols - o],
            send_sem=geo_send.at[o], recv_sem=geo_recv.at[cols - o],
            device_id=col_peer(o), device_id_type=MESH,
        )

    def copy_pay(k):
        return pltpu.make_async_remote_copy(
            src_ref=pay.at[0, 0], dst_ref=pay.at[0, k],
            send_sem=pay_send.at[k], recv_sem=pay_recv.at[k],
            device_id=line_peer(k), device_id_type=MESH,
        )

    def copy_fwd(s, k):
        return pltpu.make_async_remote_copy(
            src_ref=pay.at[0, k], dst_ref=pay.at[subs - s, k],
            send_sem=fwd_send.at[s, k], recv_sem=fwd_recv.at[subs - s, k],
            device_id={"sub": lax.rem(sub + s, subs)}, device_id_type=MESH,
        )

    def copy_sum(o):
        return pltpu.make_async_remote_copy(
            src_ref=partial.at[o], dst_ref=landed.at[o],
            send_sem=sum_send.at[o], recv_sem=sum_recv.at[o],
            device_id=col_peer(o), device_id_type=MESH,
        )

    def order(index):
        odd = index % 2
        return odd * ((index + 1) // 2) + (1 - odd) * ((rows - index // 2) % rows)

    for o in range(1, cols):
        copy_geo(o).start()
    for index in range(1, rows):
        copy_pay(order(index)).start()
    for s in range(1, subs):
        copy_fwd(s, 0).start()

    def prepare(s, k):
        columns[s, k] = jnp.concatenate(
            [pay[s, k, rank:, :]] * (128 // GEO_ROWS), axis=0
        ).T
        test = pay[s, k, :rank, :]
        high = test.astype(jnp.bfloat16)
        halves[s, k, :rank, :] = high
        halves[s, k, rank:, :] = (test - high.astype(jnp.float32)).astype(jnp.bfloat16)

    def block(s, k, o):
        xs, ys = columns[s, k, :, 0:1], columns[s, k, :, 1:2]
        zs, es = columns[s, k, :, 2:3], columns[s, k, :, 3:4]
        xt, yt = tgeo[o, 0:1, :], tgeo[o, 1:2, :]
        zt, et = tgeo[o, 2:3, :], tgeo[o, 3:4, :]
        cross = xs * xt + ys * yt
        distance = (es + et) - cross - zs * zt
        kernel = (cross + OFFSET) * lax.rsqrt(distance)
        high = kernel.astype(jnp.bfloat16)
        low = (kernel - high.astype(jnp.float32)).astype(jnp.bfloat16)
        both = jnp.dot(halves[s, k], high, preferred_element_type=jnp.float32)
        rest = jnp.dot(halves[s, k, :rank, :], low, preferred_element_type=jnp.float32)
        partial[o] += both[:rank] + (both[rank:] + rest)

    late = max(rows - 2, 0)

    @pl.loop(0, rows)
    def _(index):
        k = order(index)

        @pl.when(index > 0)
        def _():
            copy_pay(k).wait_recv()
            for s in range(1, subs):
                copy_fwd(s, k).start()

        @pl.when(index == 0)
        def _():
            for o in range(1, cols):
                copy_geo(cols - o).wait_recv()

        @pl.loop(0, subs)
        def _(s):
            @pl.when(s > 0)
            def _():
                copy_fwd(subs - s, k).wait_recv()

            prepare(s, k)

            @pl.loop(1, cols)
            def _(o):
                block(s, k, o)

            @pl.when(index < late)
            def _():
                block(s, k, 0)

    for o in range(1, cols):
        copy_sum(o).start()

    @pl.loop(late, rows)
    def _(index):
        @pl.loop(0, subs)
        def _(s):
            block(s, order(index), 0)

    sketch = partial[0]
    for o in range(1, cols):
        copy_sum(o).wait_recv()
        sketch = sketch + landed[o]
    sketch_ref[...] = sketch

    gram = lax.dot_general(
        sketch, sketch, (((1,), (1,)), ((), ())),
        precision=lax.Precision.HIGHEST, preferred_element_type=jnp.float32,
    )
    place = col * subs + sub
    gram_plane[place] = jnp.concatenate([gram[: rank // 2], gram[rank // 2 :]], axis=1)

    def copy_gp(o):
        return pltpu.make_async_remote_copy(
            src_ref=gram_plane.at[place], dst_ref=gram_plane.at[place],
            send_sem=gp_send.at[o], recv_sem=gp_recv.at[o],
            device_id=plane_peer(o), device_id_type=MESH,
        )

    def copy_gl(k):
        return pltpu.make_async_remote_copy(
            src_ref=gram_line.at[row], dst_ref=gram_line.at[row],
            send_sem=gl_send.at[k], recv_sem=gl_recv.at[k],
            device_id=line_peer(k), device_id_type=MESH,
        )

    for o in reversed(range(1, plane)):
        copy_gp(o).start()
    for o in range(1, plane):
        copy_gp(o).wait_recv()
    total = gram_plane[0]
    for o in range(1, plane):
        total = total + gram_plane[o]
    gram_line[row] = total
    for k in range(1, rows):
        copy_gl(k).start()
    for o in range(1, plane):
        copy_gp(o).wait_send()
    for o in range(1, cols):
        copy_geo(o).wait_send()
        copy_sum(o).wait_send()
    for k in range(1, rows):
        copy_pay(k).wait_send()
    for s in range(1, subs):
        for k in range(rows):
            copy_fwd(s, k).wait_send()
    for k in range(1, rows):
        copy_gl(k).wait_recv()
    total = gram_line[0]
    for k in range(1, rows):
        total = total + gram_line[k]
    gram_ref[...] = total
    for k in range(1, rows):
        copy_gl(k).wait_send()


def factor_kernel(scale, sketch_ref, gram_ref, basis_ref, factor_ref):
    rank = gram_ref.shape[1] // 2
    tiles = rank // 8
    eye = (
        lax.broadcasted_iota(jnp.int32, (rank, rank), 0)
        == lax.broadcasted_iota(jnp.int32, (rank, rank), 1)
    ).astype(jnp.float32)
    gram = jnp.concatenate([gram_ref[:, :rank], gram_ref[:, rank:]], axis=0)
    wide = jnp.concatenate([gram, eye], axis=1)
    parts = [wide[8 * t : 8 * t + 8] for t in range(tiles)]
    for own in range(tiles):
        base = 8 * own
        lines = [jnp.broadcast_to(parts[own][a : a + 1], (8, 2 * rank)) for a in range(8)]
        inner = {
            (a, b): jnp.broadcast_to(lines[a][:, base + b : base + b + 1], (8, 2 * rank))
            for a in range(8)
            for b in range(a, 8)
        }
        ratio = {}
        for a in range(8):
            inverse = 1.0 / inner[a, a]
            for b in range(a + 1, 8):
                ratio[a, b] = inner[a, b] * inverse
                for c in range(b, 8):
                    inner[b, c] = inner[b, c] - ratio[a, b] * inner[a, c]
                lines[b] = lines[b] - ratio[a, b] * lines[a]
            ratio[a, a] = inverse
        scaled = [lines[a] * ratio[a, a] for a in range(8)]
        for t in range(own + 1, tiles):
            heads = [
                jnp.broadcast_to(parts[t][:, base + a : base + a + 1], (8, 2 * rank))
                for a in range(8)
            ]
            for a in range(8):
                for b in range(a + 1, 8):
                    heads[b] = heads[b] - ratio[a, b] * heads[a]
            terms = [heads[a] * scaled[a] for a in range(8)]
            while len(terms) > 1:
                terms = [terms[i] + terms[i + 1] for i in range(0, len(terms), 2)]
            parts[t] = parts[t] - terms[0]
        parts[own] = jnp.concatenate([lines[a][a : a + 1] for a in range(8)], axis=0)
    wide = jnp.concatenate(parts, axis=0)
    pivots = jnp.sum(wide[:, :rank] * eye, axis=1, keepdims=True)
    wide = wide * lax.rsqrt(pivots)
    upper = (
        lax.broadcasted_iota(jnp.int32, (rank, rank), 0)
        <= lax.broadcasted_iota(jnp.int32, (rank, rank), 1)
    )
    factor_ref[...] = jnp.where(upper, wide[:, :rank], 0.0) * (FOLDED / scale)
    basis_ref[...] = jnp.dot(
        wide[:, rank:] * scale, sketch_ref[...],
        precision=lax.Precision.HIGHEST, preferred_element_type=jnp.float32,
    )


def per_device(filament_slot, wire_radius, strand_radius, test_matrix):
    dims = tuple(lax.axis_size(name) for name in ("row", "col", "sub"))
    rows, cols, subs = dims
    plane = cols * subs
    rank, count = test_matrix.shape
    vmem = pl.BlockSpec(memory_space=pltpu.VMEM)
    hbm = pl.BlockSpec(memory_space=pltpu.HBM)
    f32 = jnp.float32
    dma = pltpu.SemaphoreType.DMA
    sketch, gram = pl.pallas_call(
        functools.partial(sketch_kernel, dims),
        out_shape=(
            jax.ShapeDtypeStruct((rank, count), f32),
            jax.ShapeDtypeStruct((rank // 2, 2 * rank), f32),
        ),
        in_specs=[hbm] * 4,
        out_specs=(vmem, vmem),
        scratch_shapes=[
            pltpu.VMEM((1, count), jnp.int32),
            pltpu.VMEM((1, count), f32),
            pltpu.VMEM((1, strand_radius.shape[0]), f32),
            pltpu.VMEM((subs, rows, rank + GEO_ROWS, count), f32),
            pltpu.VMEM((cols, GEO_ROWS, count), f32),
            pltpu.VMEM((subs, rows, count, 128), f32),
            pltpu.VMEM((subs, rows, 2 * rank, count), jnp.bfloat16),
            pltpu.VMEM((cols, rank, count), f32),
            pltpu.VMEM((cols, rank, count), f32),
            pltpu.VMEM((plane, rank // 2, 2 * rank), f32),
            pltpu.VMEM((rows, rank // 2, 2 * rank), f32),
            dma((4,)),
            dma((rows,)), dma((rows,)), dma((subs, rows)), dma((subs, rows)),
            dma((cols,)), dma((cols,)), dma((cols,)), dma((cols,)),
            dma((plane,)), dma((plane,)), dma((rows,)), dma((rows,)),
        ],
        compiler_params=pltpu.CompilerParams(
            collective_id=0, has_side_effects=True, vmem_limit_bytes=48 * 1024 * 1024
        ),
    )(
        filament_slot.reshape(1, count),
        wire_radius.reshape(1, count),
        strand_radius.reshape(1, -1),
        test_matrix,
    )
    scale = math.sqrt(count * rows * plane)
    return pl.pallas_call(
        functools.partial(factor_kernel, scale),
        out_shape=(
            jax.ShapeDtypeStruct((rank, count), f32),
            jax.ShapeDtypeStruct((rank, rank), f32),
        ),
        in_specs=[vmem] * 2,
        out_specs=(vmem, vmem),
        compiler_params=pltpu.CompilerParams(vmem_limit_bytes=16 * 1024 * 1024),
    )(sketch, gram)


def solution(mesh):
    return jax.shard_map(
        per_device,
        mesh=mesh,
        in_specs=(
            P(("grp", "row", "col", "sub")),
            P(("grp", "row", "col", "sub")),
            P("grp"),
            P(None, ("grp", "row", "col", "sub")),
        ),
        out_specs=(P(None, ("grp", "row", "col", "sub")), P("grp", None)),
        check_vma=False,
    )
```

time: 45.5 us -> 41.5 us (0.912)
  Pallas kernels: 43.1 us -> 39.1 us
    pallas_call x1, Pallas kernels: 6.41 us -> 3.03 us  [per_device(): pl.pallas_call(functools.partial(factor_kernel, scale), out_shape=(jax.Sh...]
    pallas_call x1, Pallas kernels: 36.7 us -> 36.1 us  [per_device(): pl.pallas_call(functools.partial(sketch_kernel, dims), out_shape=(jax.Sha...]
where the time goes in v2:
time: 41.5 us; the launch traced here: 41.4 us
  Pallas kernels  39.1 us (94%)
  local copies, waits for them, and re-layouts  1.58 us (4%)
  between operations  0.66 us (2%)
    pallas_call x1, Pallas kernels, per_device(): pl.pallas_call(functools.partial(sketch_kernel, dims), out_shape=(jax.Sha...  36.1 us
    pallas_call x1, Pallas kernels, per_device(): pl.pallas_call(functools.partial(factor_kernel, scale), out_shape=(jax.Sh...  3.03 us
    unnamed x8, local copies, waits for them, and re-layouts  1.58 us

profile of v2, /device:TPU:0, one launch (start us, length us, event | category | flops | bytes accessed | tf_op | source)
XLA Modules:
  0.0 41.4 jit_solution(11580045741680554957)
XLA Ops:
  0.6 0.0 copy-start.2
  0.6 0.0 copy-start.1
  0.7 0.0 copy-start.3
  0.7 0.7 %copy-done.2 = f32[512]{0:T(512)S(1)} copy-done((f32[512]{0:T(512)S(1)}, f32[512]{0:T(512)}, u32[]{:S(2)}) %copy-start.2) | copy-done | bytes 2072
  1.3 0.0 copy-done.1
  1.3 0.0 copy-done.3
  1.3 0.0 copy-start
  1.3 0.9 %copy-done = f32[64,512]{1,0:T(8,128)S(1)} copy-done((f32[64,512]{1,0:T(8,128)S(1)}, f32[64,512]{1,0:T(8,128)}, u32[]{:S(2)}) %copy-start) | copy-done | bytes 131096
  2.2 36.1 %shard_map.59 = (f32[64,512]{1,0:T(8,128)S(1)}, f32[32,128]{1,0:T(8,128)S(1)}) custom-call(s32[1,512]{1,0:T(1,128)S(1)} %bitcast.3, f32[1,512]{1,0:T(1,128)S(1)} %bitcast.4, f32[1,64]{1,0:T(1,128)S(1)} %bitcast.5, f32[64,512]{1,0:T(8,128)S(1)} %copy-done), custom_call_target="tpu_custom_call" | custom-call | tf_op jit(solution)/shard_map/pallas_call | solution.py:316
  38.3 3.0 %shard_map.60 = (f32[64,512]{1,0:T(8,128)}, f32[64,64]{1,0:T(8,128)}) custom-call(f32[64,512]{1,0:T(8,128)S(1)} %get-tuple-element.4.sketch_ref, f32[32,128]{1,0:T(8,128)S(1)} %get-tuple-element.5.gram_ref), custom_call_target="tpu_custom_call" | custom-call | tf_op jit(solution)/shard_map/pallas_call | solution.py:351
Async XLA Ops:
  0.6 0.7 %copy-start.2 = (f32[512]{0:T(512)S(1)}, f32[512]{0:T(512)}, u32[]{:S(2)}) copy-start(f32[512]{0:T(512)} %param.5) | copy-start | bytes 6148
  0.6 0.7 %copy-start.1 = (s32[512]{0:T(512)S(1)}, s32[512]{0:T(512)}, u32[]{:S(2)}) copy-start(s32[512]{0:T(512)} %param.4) | copy-start | bytes 6148
  0.7 0.7 %copy-start.3 = (f32[64]{0:T(128)S(1)}, f32[64]{0:T(128)}, u32[]{:S(2)}) copy-start(f32[64]{0:T(128)} %param.6) | copy-start | bytes 772
  1.3 0.9 %copy-start = (f32[64,512]{1,0:T(8,128)S(1)}, f32[64,512]{1,0:T(8,128)}, u32[]{:S(2)}) copy-start(f32[64,512]{1,0:T(8,128)} %test_hbm.1) | copy-start | bytes 393220

commit v3 on v2

--- a/solution.py
+++ b/solution.py
@@ -41,6 +41,11 @@
     return jnp.concatenate([x, y, z, e, x, y, z, e], axis=0)
 
 
+def split_rows(rows):
+    count = 2 if rows % 2 == 0 else 1
+    return rows // count, count
+
+
 def sketch_kernel(
     dims, slot_hbm, wire_hbm, radius_hbm, test_hbm, sketch_ref, gram_ref,
     slot_ref, wire_ref, radius_ref,
@@ -50,6 +55,8 @@
 ):
     rows, cols, subs = dims
     plane = cols * subs
+    near, halves_count = split_rows(rows)
+    line = near * cols
     rank, count = test_hbm.shape
     row, col, sub = lax.axis_index("row"), lax.axis_index("col"), lax.axis_index("sub")
 
@@ -59,11 +66,17 @@
             "sub": lax.rem(sub + o % subs, subs),
         }
 
+    def row_peer(k):
+        return {"row": lax.rem(row + k, rows)}
+
     def line_peer(k):
-        return {"row": lax.rem(row + k, rows)}
-
-    def col_peer(o):
-        return {"col": lax.rem(col + o, cols)}
+        return {
+            "row": row // near * near + lax.rem(row + k // cols, near),
+            "col": lax.rem(col + k % cols, cols),
+        }
+
+    def half_peer(o):
+        return {"row": lax.rem(row + o * near, rows)}
 
     loads = [
         pltpu.make_async_copy(slot_hbm, slot_ref, load_sem.at[0]),
@@ -77,6 +90,9 @@
     for o in range(1, plane):
         pl.semaphore_signal(barrier, inc=1, device_id=plane_peer(o), device_id_type=MESH)
     for k in range(1, rows):
+        pl.semaphore_signal(barrier, inc=1, device_id=row_peer(k), device_id_type=MESH)
+    across = [k for k in range(1, line) if k // cols and k % cols]
+    for k in across:
         pl.semaphore_signal(barrier, inc=1, device_id=line_peer(k), device_id_type=MESH)
 
     for load in loads[:3]:
@@ -86,13 +102,13 @@
     tgeo[0] = geo
     partial[...] = jnp.zeros_like(partial)
     loads[3].wait()
-    pl.semaphore_wait(barrier, plane + rows - 2)
+    pl.semaphore_wait(barrier, plane + rows - 2 + len(across))
 
     def copy_geo(o):
         return pltpu.make_async_remote_copy(
-            src_ref=pay.at[0, 0, pl.ds(rank, GEO_ROWS)], dst_ref=tgeo.at[cols - o],
-            send_sem=geo_send.at[o], recv_sem=geo_recv.at[cols - o],
-            device_id=col_peer(o), device_id_type=MESH,
+            src_ref=pay.at[0, 0, pl.ds(rank, GEO_ROWS)], dst_ref=tgeo.at[halves_count - o],
+            send_sem=geo_send.at[o], recv_sem=geo_recv.at[halves_count - o],
+            device_id=half_peer(o), device_id_type=MESH,
         )
 
     def copy_pay(k):
@@ -113,17 +129,13 @@
         return pltpu.make_async_remote_copy(
             src_ref=partial.at[o], dst_ref=landed.at[o],
             send_sem=sum_send.at[o], recv_sem=sum_recv.at[o],
-            device_id=col_peer(o), device_id_type=MESH,
-        )
-
-    def order(index):
-        odd = index % 2
-        return odd * ((index + 1) // 2) + (1 - odd) * ((rows - index // 2) % rows)
-
-    for o in range(1, cols):
+            device_id=half_peer(o), device_id_type=MESH,
+        )
+
+    for o in range(1, halves_count):
         copy_geo(o).start()
-    for index in range(1, rows):
-        copy_pay(order(index)).start()
+    for k in range(1, line):
+        copy_pay(k).start()
     for s in range(1, subs):
         copy_fwd(s, 0).start()
 
@@ -150,22 +162,20 @@
         rest = jnp.dot(halves[s, k, :rank, :], low, preferred_element_type=jnp.float32)
         partial[o] += both[:rank] + (both[rank:] + rest)
 
-    late = max(rows - 2, 0)
-
-    @pl.loop(0, rows)
-    def _(index):
-        k = order(index)
-
-        @pl.when(index > 0)
+    late = 1
+
+    @pl.loop(0, line)
+    def _(k):
+        @pl.when(k > 0)
         def _():
             copy_pay(k).wait_recv()
             for s in range(1, subs):
                 copy_fwd(s, k).start()
 
-        @pl.when(index == 0)
+        @pl.when(k == 0)
         def _():
-            for o in range(1, cols):
-                copy_geo(cols - o).wait_recv()
+            for o in range(1, halves_count):
+                copy_geo(halves_count - o).wait_recv()
 
         @pl.loop(0, subs)
         def _(s):
@@ -175,25 +185,25 @@
 
             prepare(s, k)
 
-            @pl.loop(1, cols)
+            @pl.loop(1, halves_count)
             def _(o):
                 block(s, k, o)
 
-            @pl.when(index < late)
+            @pl.when(k < late)
             def _():
                 block(s, k, 0)
 
-    for o in range(1, cols):
+    for o in range(1, halves_count):
         copy_sum(o).start()
 
-    @pl.loop(late, rows)
-    def _(index):
+    @pl.loop(late, line)
+    def _(k):
         @pl.loop(0, subs)
         def _(s):
-            block(s, order(index), 0)
+            block(s, k, 0)
 
     sketch = partial[0]
-    for o in range(1, cols):
+    for o in range(1, halves_count):
         copy_sum(o).wait_recv()
         sketch = sketch + landed[o]
     sketch_ref[...] = sketch
@@ -216,7 +226,7 @@
         return pltpu.make_async_remote_copy(
             src_ref=gram_line.at[row], dst_ref=gram_line.at[row],
             send_sem=gl_send.at[k], recv_sem=gl_recv.at[k],
-            device_id=line_peer(k), device_id_type=MESH,
+            device_id=row_peer(k), device_id_type=MESH,
         )
 
     for o in reversed(range(1, plane)):
@@ -231,13 +241,13 @@
         copy_gl(k).start()
     for o in range(1, plane):
         copy_gp(o).wait_send()
-    for o in range(1, cols):
+    for o in range(1, halves_count):
         copy_geo(o).wait_send()
         copy_sum(o).wait_send()
-    for k in range(1, rows):
+    for k in range(1, line):
         copy_pay(k).wait_send()
     for s in range(1, subs):
-        for k in range(rows):
+        for k in range(line):
             copy_fwd(s, k).wait_send()
     for k in range(1, rows):
         copy_gl(k).wait_recv()
@@ -308,11 +318,14 @@
     dims = tuple(lax.axis_size(name) for name in ("row", "col", "sub"))
     rows, cols, subs = dims
     plane = cols * subs
+    near, halves_count = split_rows(rows)
+    line = near * cols
     rank, count = test_matrix.shape
     vmem = pl.BlockSpec(memory_space=pltpu.VMEM)
     hbm = pl.BlockSpec(memory_space=pltpu.HBM)
     f32 = jnp.float32
     dma = pltpu.SemaphoreType.DMA
+    keep = pltpu.with_memory_space_constraint
     sketch, gram = pl.pallas_call(
         functools.partial(sketch_kernel, dims),
         out_shape=(
@@ -325,27 +338,27 @@
             pltpu.VMEM((1, count), jnp.int32),
             pltpu.VMEM((1, count), f32),
             pltpu.VMEM((1, strand_radius.shape[0]), f32),
-            pltpu.VMEM((subs, rows, rank + GEO_ROWS, count), f32),
-            pltpu.VMEM((cols, GEO_ROWS, count), f32),
-            pltpu.VMEM((subs, rows, count, 128), f32),
-            pltpu.VMEM((subs, rows, 2 * rank, count), jnp.bfloat16),
-            pltpu.VMEM((cols, rank, count), f32),
-            pltpu.VMEM((cols, rank, count), f32),
+            pltpu.VMEM((subs, line, rank + GEO_ROWS, count), f32),
+            pltpu.VMEM((halves_count, GEO_ROWS, count), f32),
+            pltpu.VMEM((subs, line, count, 128), f32),
+            pltpu.VMEM((subs, line, 2 * rank, count), jnp.bfloat16),
+            pltpu.VMEM((halves_count, rank, count), f32),
+            pltpu.VMEM((halves_count, rank, count), f32),
             pltpu.VMEM((plane, rank // 2, 2 * rank), f32),
             pltpu.VMEM((rows, rank // 2, 2 * rank), f32),
             dma((4,)),
-            dma((rows,)), dma((rows,)), dma((subs, rows)), dma((subs, rows)),
-            dma((cols,)), dma((cols,)), dma((cols,)), dma((cols,)),
+            dma((line,)), dma((line,)), dma((subs, line)), dma((subs, line)),
+            dma((halves_count,)), dma((halves_count,)), dma((halves_count,)), dma((halves_count,)),
             dma((plane,)), dma((plane,)), dma((rows,)), dma((rows,)),
         ],
         compiler_params=pltpu.CompilerParams(
             collective_id=0, has_side_effects=True, vmem_limit_bytes=48 * 1024 * 1024
         ),
     )(
-        filament_slot.reshape(1, count),
-        wire_radius.reshape(1, count),
-        strand_radius.reshape(1, -1),
-        test_matrix,
+        keep(filament_slot.reshape(1, count), pltpu.HBM),
+        keep(wire_radius.reshape(1, count), pltpu.HBM),
+        keep(strand_radius.reshape(1, -1), pltpu.HBM),
+        keep(test_matrix, pltpu.HBM),
     )
     scale = math.sqrt(count * rows * plane)
     return pl.pallas_call(

time: 41.5 us -> 36.9 us (0.89)
  Pallas kernels: 39.1 us -> 36.1 us
  local copies, waits for them, and re-layouts: 1.58 us -> 0 us
    pallas_call x1, Pallas kernels: 36.1 us -> 33.1 us  [per_device(): pl.pallas_call(functools.partial(sketch_kernel, dims), out_shape=(jax.Sha...]
    unnamed x8 -> x0, local copies, waits for them, and re-layouts: 1.58 us -> none
where the time goes in v3:
time: 36.9 us; the launch traced here: 36.7 us
  Pallas kernels  36.1 us (98%)
  between operations  0.64 us (2%)
    pallas_call x1, Pallas kernels, per_device(): pl.pallas_call(functools.partial(sketch_kernel, dims), out_shape=(jax.Sha...  33.1 us
    pallas_call x1, Pallas kernels, per_device(): pl.pallas_call(functools.partial(factor_kernel, scale), out_shape=(jax.Sh...  3.03 us

profile of v3, /device:TPU:0, one launch (start us, length us, event | category | flops | bytes accessed | tf_op | source)
XLA Modules:
  0.0 36.7 jit_solution(43714123201972619)
XLA Ops:
  0.6 33.1 %shard_map.59 = (f32[64,512]{1,0:T(8,128)S(1)}, f32[32,128]{1,0:T(8,128)S(1)}) custom-call(s32[1,512]{1,0:T(1,128)} %bitcast.3, f32[1,512]{1,0:T(1,128)} %bitcast.4, f32[1,64]{1,0:T(1,128)} %bitcast.5, f32[64,512]{1,0:T(8,128)} %test_hbm.1), custom_call_target="tpu_custom_call" | custom-call | tf_op jit(solution)/shard_map/pallas_call | solution.py:329
  33.7 3.0 %shard_map.60 = (f32[64,512]{1,0:T(8,128)}, f32[64,64]{1,0:T(8,128)}) custom-call(f32[64,512]{1,0:T(8,128)S(1)} %get-tuple-element.4.sketch_ref, f32[32,128]{1,0:T(8,128)S(1)} %get-tuple-element.5.gram_ref), custom_call_target="tpu_custom_call" | custom-call | tf_op jit(solution)/shard_map/pallas_call | solution.py:364

commit v4 on v3

--- a/solution.py
+++ b/solution.py
@@ -149,20 +149,20 @@
         halves[s, k, rank:, :] = (test - high.astype(jnp.float32)).astype(jnp.bfloat16)
 
     def block(s, k, o):
-        xs, ys = columns[s, k, :, 0:1], columns[s, k, :, 1:2]
-        zs, es = columns[s, k, :, 2:3], columns[s, k, :, 3:4]
-        xt, yt = tgeo[o, 0:1, :], tgeo[o, 1:2, :]
-        zt, et = tgeo[o, 2:3, :], tgeo[o, 3:4, :]
-        cross = xs * xt + ys * yt
-        distance = (es + et) - cross - zs * zt
-        kernel = (cross + OFFSET) * lax.rsqrt(distance)
-        high = kernel.astype(jnp.bfloat16)
-        low = (kernel - high.astype(jnp.float32)).astype(jnp.bfloat16)
-        both = jnp.dot(halves[s, k], high, preferred_element_type=jnp.float32)
-        rest = jnp.dot(halves[s, k, :rank, :], low, preferred_element_type=jnp.float32)
-        partial[o] += both[:rank] + (both[rank:] + rest)
-
-    late = 1
+        for j in range(0, count, 256):
+            part = halves[s, k, :, j : j + 256]
+            xs, ys = columns[s, k, j : j + 256, 0:1], columns[s, k, j : j + 256, 1:2]
+            zs, es = columns[s, k, j : j + 256, 2:3], columns[s, k, j : j + 256, 3:4]
+            xt, yt = tgeo[o, 0:1, :], tgeo[o, 1:2, :]
+            zt, et = tgeo[o, 2:3, :], tgeo[o, 3:4, :]
+            cross = xs * xt + ys * yt
+            distance = (es + et) - cross - zs * zt
+            kernel = (cross + OFFSET) * lax.rsqrt(distance)
+            high = kernel.astype(jnp.bfloat16)
+            low = (kernel - high.astype(jnp.float32)).astype(jnp.bfloat16)
+            both = jnp.dot(part, high, preferred_element_type=jnp.float32)
+            rest = jnp.dot(part[:rank], low, preferred_element_type=jnp.float32)
+            partial[o, :, :] += both[:rank] + (both[rank:] + rest)
 
     @pl.loop(0, line)
     def _(k):
@@ -189,14 +189,10 @@
             def _(o):
                 block(s, k, o)
 
-            @pl.when(k < late)
-            def _():
-                block(s, k, 0)
-
     for o in range(1, halves_count):
         copy_sum(o).start()
 
-    @pl.loop(late, line)
+    @pl.loop(0, line)
     def _(k):
         @pl.loop(0, subs)
         def _(s):

time: 36.9 us -> 35 us (0.949)
  Pallas kernels: 36.1 us -> 34.2 us
    pallas_call x1, Pallas kernels: 33.1 us -> 31.2 us  [per_device(): pl.pallas_call(functools.partial(sketch_kernel, dims), out_shape=(jax.Sha...]
where the time goes in v4:
time: 35 us; the launch traced here: 34.9 us
  Pallas kernels  34.2 us (98%)
  between operations  0.64 us (2%)
    pallas_call x1, Pallas kernels, per_device(): pl.pallas_call(functools.partial(sketch_kernel, dims), out_shape=(jax.Sha...  31.2 us
    pallas_call x1, Pallas kernels, per_device(): pl.pallas_call(functools.partial(factor_kernel, scale), out_shape=(jax.Sh...  3.03 us

profile of v4, /device:TPU:0, one launch (start us, length us, event | category | flops | bytes accessed | tf_op | source)
XLA Modules:
  0.0 34.9 jit_solution(7471510571802882891)
XLA Ops:
  0.6 31.2 %shard_map.59 = (f32[64,512]{1,0:T(8,128)S(1)}, f32[32,128]{1,0:T(8,128)S(1)}) custom-call(s32[1,512]{1,0:T(1,128)} %bitcast.3, f32[1,512]{1,0:T(1,128)} %bitcast.4, f32[1,64]{1,0:T(1,128)} %bitcast.5, f32[64,512]{1,0:T(8,128)} %test_hbm.1), custom_call_target="tpu_custom_call" | custom-call | tf_op jit(solution)/shard_map/pallas_call | solution.py:325
  31.9 3.0 %shard_map.60 = (f32[64,512]{1,0:T(8,128)}, f32[64,64]{1,0:T(8,128)}) custom-call(f32[64,512]{1,0:T(8,128)S(1)} %get-tuple-element.4.sketch_ref, f32[32,128]{1,0:T(8,128)S(1)} %get-tuple-element.5.gram_ref), custom_call_target="tpu_custom_call" | custom-call | tf_op jit(solution)/shard_map/pallas_call | solution.py:360
